TPU v7x, 512 devices: a whole 4x8x8 slice. The times are simulated.
512 devices in a mesh: rows: 8 (over z), cols: 8 (over y), depth: 8 (over x, core).
Axes of the slice: x: 4, y: 8, z: 8, core: 2. Of those that a mesh axis runs over, the one named last changes fastest.
Arguments:
- tokens: bfloat16 [512, 12288], P(('rows', 'cols'), 'depth'), may hold values from -6 to 6
- weight_in: bfloat16 [12288, 49152], P('depth', ('rows', 'cols')), may hold values from -0.0546875 to 0.0546875
- bias_in: float32 [49152], P(('rows', 'cols')), may hold values from -4 to 4
- weight_out: bfloat16 [49152, 12288], P(('rows', 'cols'), 'depth'), may hold values from -0.02734375 to 0.02734375
- bias_out: float32 [12288], P('depth'), may hold values from -3 to 3
Outputs:
- output: bfloat16 [512, 12288], P(('rows', 'cols'), 'depth')
All inputs are finite; a program needn't handle non-finite values.
Results may differ from a plain program's by a relative error of at most 0.0046.
Values may be sent and summed in bfloat16 or wider, within the bound.
No kernel may reach another device: no remote copies, remote signals or barrier semaphores. Data moves between devices by JAX's collectives and lax.ppermute only.
A program may use at most 64 MiB of HBM per device.

v0:
```python
import jax
import jax.numpy as jnp
from jax import lax
from jax.sharding import PartitionSpec as P


def shards(tokens, weight_in, bias_in, weight_out, bias_out):
    partial_value = jnp.dot(
        lax.all_gather(tokens, ("rows", "cols"), axis=0, tiled=True),
        weight_in,
        preferred_element_type=jnp.float32,
    )
    total = lax.psum(partial_value, "depth")
    active = jax.nn.gelu(total + bias_in, approximate=True).astype(jnp.bfloat16)
    summed = lax.psum_scatter(
        jnp.dot(active, weight_out, preferred_element_type=jnp.float32),
        ("rows", "cols"),
        scatter_dimension=0,
        tiled=True,
    )
    return (summed + bias_out).astype(jnp.bfloat16)


def solution(mesh):
    in_specs = (
        P(("rows", "cols"), "depth"),
        P("depth", ("rows", "cols")),
        P(("rows", "cols")),
        P(("rows", "cols"), "depth"),
        P("depth"),
    )
    out_specs = P(("rows", "cols"), "depth")
    return jax.shard_map(shards, mesh=mesh, in_specs=in_specs, out_specs=out_specs, check_vma=False)
```

profile of v0, /device:TPU:2, one launch (start us, length us, event | category | flops | bytes accessed | tf_op | source)
XLA Modules:
  0.0 353.3 jit_solution(1478955682102614328)
XLA Ops:
  6.5 0.0 copy-start
  6.5 0.0 all-gather.2.cloned.1.call-start
  6.5 0.7 all-gather.2.cloned.1.call-update
  7.3 0.0 all-reduce.4.cloned.1.call-start
  7.3 90.5 %all-gather.2.cloned.1.call-done = bf16[512,1536]{1,0:T(8,128)(2,1)} async-done(((bf16[8,1536]{1,0:T(8,128)(2,1)}), bf16[512,1536]{1,0:T(8,128)(2,1)}) %all-gather.2.cloned.1.call-update) | async-done | bytes 1572880 | tf_op jit(solution)/shard_map/all_gather | solution.py:9
  97.8 4.7 %fusion.20 = f32[512,768]{1,0:T(8,128)} fusion(bf16[512,1536]{1,0:T(8,128)(2,1)} %all-gather.2.cloned.1.call-done, bf16[1536,768]{1,0:T(8,128)(2,1)} %param.6), kind=kOutput, calls=%fused_computation.21 | convolution fusion | flops 1207959552 | bytes 5505024 | tf_op jit(solution)/shard_map/dot_general | solution.py:8
  102.5 0.0 copy-start.2
  102.5 0.0 all-reduce.4.cloned.1.call-update
  102.5 0.0 all-reduce.6.cloned.1.call-start
  102.6 69.5 %all-reduce.4.cloned.1.call-done = f32[512,768]{1,0:T(8,128)} async-done(((f32[512,768]{1,0:T(8,128)}), f32[512,768]{1,0:T(8,128)}) %all-reduce.4.cloned.1.call-update) | async-done | bytes 1572880 | tf_op jit(solution)/shard_map/psum | solution.py:13
  172.1 0.0 copy-done
  172.1 0.0 copy-done.2
  172.1 4.6 %fusion.8 = f32[512,1536]{1,0:T(8,128)} fusion(bf16[768,1536]{1,0:T(8,128)(2,1)S(1)} %copy-done, f32[512,768]{1,0:T(8,128)} %all-reduce.4.cloned.1.call-done, f32[768]{0:T(1024)S(1)} %copy-done.2), kind=kOutput, calls=%fused_computation.9 | convolution fusion | flops 1211891712 | bytes 7080960 | tf_op jit(solution)/shard_map/dot_general | solution.py:16
  176.7 0.0 copy-start.1
  176.7 0.0 all-reduce.6.cloned.1.call-update
  176.7 1.3 dynamic-slice
  178.6 166.8 %all-reduce.6.cloned.1.call-done = f32[512,1536]{1,0:T(8,128)} async-done(((f32[512,1536]{1,0:T(8,128)}), f32[512,1536]{1,0:T(8,128)}) %all-reduce.6.cloned.1.call-update) | async-done | bytes 3145744
  345.4 0.0 copy-done.1
  345.4 1.4 fusion.15
Async XLA Ops:
  6.5 165.5 %copy-start = (bf16[768,1536]{1,0:T(8,128)(2,1)S(1)}, bf16[768,1536]{1,0:T(8,128)(2,1)}, u32[]{:S(2)}) copy-start(bf16[768,1536]{1,0:T(8,128)(2,1)} %param.8) | copy-start | bytes 7077892
  6.5 91.3 %all-gather.2.cloned.1.call-start = ((), (), s32[]{:S(2)}) async-start(), calls=%async_computation | async-start | bytes 1597440 | tf_op jit(solution)/shard_map/all_gather | solution.py:9
  7.3 164.8 %all-reduce.4.cloned.1.call-start = ((), (), s32[]{:S(2)}) async-start(), calls=%async_computation.1 | async-start | bytes 3145728 | tf_op jit(solution)/shard_map/psum | solution.py:13
  102.5 69.6 %copy-start.2 = (f32[768]{0:T(1024)S(1)}, f32[768]{0:T(1024)}, u32[]{:S(2)}) copy-start(f32[768]{0:T(1024)} %param.7) | copy-start | bytes 9220
  102.5 242.8 %all-reduce.6.cloned.1.call-start = ((), (), s32[]{:S(2)}) async-start(), calls=%async_computation.2 | async-start | bytes 6291456
  176.7 168.7 %copy-start.1 = (f32[1536]{0:T(1024)S(1)}, f32[1536]{0:T(1024)}, u32[]{:S(2)}) copy-start(f32[1536]{0:T(1024)} %param.9) | copy-start | bytes 18436
Sparse Core Ops, SparseCore 0:
  10.4 87.4 all-gather.1
  102.6 69.3 all-reduce.3
  176.8 168.5 all-reduce.5
where the time goes:
time: 354 us; the launch traced here: 353 us
  waiting for transfers between devices  327 us (92%)
  between operations  13.8 us (4%)
  matrix products  9.27 us (3%)
    unnamed x4, waiting for transfers between devices  167 us
    all_gather x1, waiting for transfers between devices, shards(): lax.all_gather(tokens, ('rows', 'cols'), axis=0, tiled=True)  90.5 us
    psum x1, waiting for transfers between devices, shards(): total = lax.psum(partial_value, 'depth')  69.5 us
  transfers between devices with their start and end apart: 3, of which 3 were waited for; matrix products, arithmetic and copies ran while one was open for 0% of the time, Pallas kernels for 0%

commit v1 on v0

--- a/solution.py
+++ b/solution.py
@@ -6,7 +6,15 @@
 
 def shards(tokens, weight_in, bias_in, weight_out, bias_out):
     partial_value = jnp.dot(
-        lax.all_gather(tokens, ("rows", "cols"), axis=0, tiled=True),
+        jnp.concatenate(
+            lax.all_to_all(
+                jnp.stack([tokens for _ in range(lax.axis_size(("rows", "cols")))], axis=0),
+                axis_name=("rows", "cols"),
+                split_axis=0,
+                concat_axis=0,
+            ),
+            axis=0,
+        ),
         weight_in,
         preferred_element_type=jnp.float32,
     )

time: 354 us -> 318 us (0.90)
  waiting for transfers between devices: 327 us -> 235 us
  blocking collectives: 0 us -> 57.8 us
    all_gather x1 -> x0, waiting for transfers between devices: 90.5 us -> none  [shards(): lax.all_gather(tokens, ('rows', 'cols'), axis=0, tiled=True)]
    all_to_all x0 -> x1, blocking collectives: none -> 57.8 us  [shards(): lax.all_to_all(jnp.stack([tokens for _ in range(lax.axis_size(('rows', 'c...]
    unnamed x4 -> x3, waiting for transfers between devices: 167 us -> 167 us
  transfers between devices with their start and end apart: 3 -> 2, of which waited for: 3 -> 2; matrix products, arithmetic and copies ran while one was open for 0% -> 0% of each run, Pallas kernels for 0% -> 0%
where the time goes in v1:
time: 318 us
  waiting for transfers between devices  235 us (74%)
  blocking collectives  57.8 us (18%)
  between operations  14.1 us (4%)
  matrix products  7.13 us (2%)
    unnamed x3, waiting for transfers between devices  167 us
    psum x1, waiting for transfers between devices, shards(): total = lax.psum(partial_value, 'depth')  68.2 us
    all_to_all x1, blocking collectives, shards(): lax.all_to_all(jnp.stack([tokens for _ in range(lax.axis_size(('rows', 'c...  57.8 us
  transfers between devices with their start and end apart: 2, of which 2 were waited for; matrix products, arithmetic and copies ran while one was open for 0% of the time, Pallas kernels for 0%

profile of v1, /device:TPU:2, one launch (start us, length us, event | category | flops | bytes accessed | tf_op | source)
XLA Modules:
  0.0 317.8 jit_solution(13465338840589327875)
XLA Ops:
  6.5 0.0 copy-start
  6.5 0.0 all-reduce.4.cloned.1.call-start
  6.5 1.0 stack.2
  7.5 0.0 copy-start.2
  7.5 57.8 %all_to_all.5 = bf16[64,8,1536]{2,1,0:T(8,128)(2,1)S(1)} all-to-all(bf16[64,8,1536]{2,1,0:T(8,128)(2,1)S(1)} %stack.2), channel_id=1, replica_groups=mesh['rows'=8,'cols'=8,'depth'=8] {'rows','cols'}, dimensions={0} | all-to-all | bytes 3145728 | tf_op jit(solution)/shard_map/all_to_all | solution.py:10
  65.3 0.0 copy-done.2
  65.3 2.5 fusion.8
  67.9 0.0 copy-start.3
  67.9 0.0 all-reduce.4.cloned.1.call-update
  67.9 0.0 all-reduce.6.cloned.1.call-start
  68.0 68.2 %all-reduce.4.cloned.1.call-done = f32[512,768]{1,0:T(8,128)} async-done(((f32[512,768]{1,0:T(8,128)}), f32[512,768]{1,0:T(8,128)}) %all-reduce.4.cloned.1.call-update) | async-done | bytes 1572880 | tf_op jit(solution)/shard_map/psum | solution.py:21
  136.1 0.0 copy-done
  136.1 0.0 copy-done.3
  136.2 4.6 %fusion.10 = f32[512,1536]{1,0:T(8,128)} fusion(bf16[768,1536]{1,0:T(8,128)(2,1)S(1)} %copy-done, f32[512,768]{1,0:T(8,128)} %all-reduce.4.cloned.1.call-done, f32[768]{0:T(1024)S(1)} %copy-done.3), kind=kOutput, calls=%fused_computation.11 | convolution fusion | flops 1211891712 | bytes 7080960 | tf_op jit(solution)/shard_map/dot_general | solution.py:24
  140.7 0.0 copy-start.1
  140.7 0.0 all-reduce.6.cloned.1.call-update
  140.8 1.3 dynamic-slice
  142.7 166.8 %all-reduce.6.cloned.1.call-done = f32[512,1536]{1,0:T(8,128)} async-done(((f32[512,1536]{1,0:T(8,128)}), f32[512,1536]{1,0:T(8,128)}) %all-reduce.6.cloned.1.call-update) | async-done | bytes 3145744
  309.5 0.0 copy-done.1
  309.5 1.4 fusion.17
Async XLA Ops:
  6.5 129.6 %copy-start = (bf16[768,1536]{1,0:T(8,128)(2,1)S(1)}, bf16[768,1536]{1,0:T(8,128)(2,1)}, u32[]{:S(2)}) copy-start(bf16[768,1536]{1,0:T(8,128)(2,1)} %param.8) | copy-start | bytes 7077892
  6.5 129.6 %all-reduce.4.cloned.1.call-start = ((), (), s32[]{:S(2)}) async-start(), calls=%async_computation.1 | async-start | bytes 3145728 | tf_op jit(solution)/shard_map/psum | solution.py:21
  7.5 57.8 %copy-start.2 = (bf16[1536,768]{1,0:T(8,128)(2,1)S(1)}, bf16[1536,768]{1,0:T(8,128)(2,1)}, u32[]{:S(2)}) copy-start(bf16[1536,768]{1,0:T(8,128)(2,1)} %param.6) | copy-start | bytes 7077892
  67.9 68.3 %copy-start.3 = (f32[768]{0:T(1024)S(1)}, f32[768]{0:T(1024)}, u32[]{:S(2)}) copy-start(f32[768]{0:T(1024)} %param.7) | copy-start | bytes 9220
  67.9 241.6 %all-reduce.6.cloned.1.call-start = ((), (), s32[]{:S(2)}) async-start(), calls=%async_computation.2 | async-start | bytes 6291456
  140.7 168.8 %copy-start.1 = (f32[1536]{0:T(1024)S(1)}, f32[1536]{0:T(1024)}, u32[]{:S(2)}) copy-start(f32[1536]{0:T(1024)} %param.9) | copy-start | bytes 18436
Sparse Core Ops, SparseCore 0:
  68.0 68.0 all-reduce.3
  140.9 168.5 all-reduce.5
